TPU v7x, 256 devices: a whole 4x4x8 slice. The times are simulated.
256 devices in a mesh: tm: 4 (over y_hi, core), space: 16 (over y_lo, z), head: 4 (over x).
Axes of the slice: x: 4, y: 4 (y_hi: 2, y_lo: 2; y = y_hi * 2 + y_lo), z: 8, core: 2. Of those that a mesh axis runs over, the one named last changes fastest.
Arguments:
- queries: bfloat16 [32, 64, 32, 3072], P('tm', 'space', None, 'head'), may hold values from -6 to 6
- key_rows: bfloat16 [32, 64, 32, 3072], P('tm', 'space', None, 'head'), may hold values from -6 to 6
- value_rows: bfloat16 [32, 64, 32, 3072], P('tm', 'space', None, 'head'), may hold values from -6 to 6
- text_keys: bfloat16 [128, 3072], P('tm', 'head'), may hold values from -6 to 6
- text_values: bfloat16 [128, 3072], P('tm', 'head'), may hold values from -6 to 6
- text_count: int32 [1], replicated, may hold values from 32 to 128
- window_table: int32 [32, 64, 4], replicated, may hold values from 12 to 8191, as said below
Outputs:
- attended: bfloat16 [32, 64, 32, 3072], P('tm', 'space', None, 'head')
Inputs may be any that keep to these rules, and one draw needn't show every extreme that they name: `window_table`: each window is a box of whole tiles spanning at most two frames, at most two neighbouring row groups (rows k * 4 to (k + 1) * 4 - 1) and at most two neighbouring tiles; some window spans two in each; tiles of different windows have different ids.
All inputs are finite; a program needn't handle non-finite values.
Results may differ from a plain program's by a relative error of at most 0.0045.
Values may be sent and summed in bfloat16 or wider, within the bound.
A program may use at most 128 MiB of HBM per device.

v0:
```python
import math

import jax
import jax.numpy as jnp
from jax import lax
from jax.sharding import PartitionSpec as P

RT = 4
TILE = 8
HD = 128


def with_halo(block, sides, width):
    for axis, dim in sides:
        count = lax.axis_size(axis)
        forward = [(i, i + 1) for i in range(count - 1)]
        backward = [(target, source) for source, target in forward]
        low = lax.ppermute(
            lax.slice_in_dim(block, block.shape[dim] - width, None, axis=dim), axis, forward
        )
        high = lax.ppermute(lax.slice_in_dim(block, 0, width, axis=dim), axis, backward)
        block = jnp.concatenate([low, block, high], axis=dim)
    return block


def attend_head(query_block, key_block, value_block, allowed, score_scale, head_index):
    query_one = lax.dynamic_index_in_dim(query_block, head_index, 1, keepdims=False)
    key_one = lax.dynamic_index_in_dim(key_block, head_index, 1, keepdims=False)
    value_one = lax.dynamic_index_in_dim(value_block, head_index, 1, keepdims=False)
    scores = (
        jnp.einsum("qd,kd->qk", query_one, key_one, preferred_element_type=jnp.float32)
        * score_scale
    )
    scores = jnp.where(allowed, scores, -jnp.inf)
    highest = jnp.max(scores, axis=1, keepdims=True)
    weights = jnp.exp(scores - highest)
    denominator = jnp.sum(weights, axis=1, keepdims=True)
    weights_low = weights.astype(jnp.bfloat16)
    summed = jnp.dot(weights_low, value_one, preferred_element_type=jnp.float32)
    return (summed / denominator).astype(jnp.bfloat16)


def per_device(queries, key_rows, value_rows, text_keys, text_values, text_count, window_table):
    frame_count, row_count, col_count, feat_count = queries.shape
    head_count = feat_count // HD
    joined = jnp.concatenate([key_rows, value_rows], axis=3)
    widened = with_halo(joined, (("tm", 0),), 1)
    widened = with_halo(widened, (("space", 1),), RT)
    text_pairs = lax.all_gather(
        jnp.concatenate([text_keys, text_values], axis=1), "tm", axis=0, tiled=True
    )
    text_total = text_pairs.shape[0]
    text_pairs = text_pairs.reshape(text_total, 2, head_count, HD)
    text_allowed = jnp.arange(text_total, dtype=jnp.int32) < text_count[0]
    padded_ids = jnp.pad(window_table, ((1, 1), (RT, RT), (0, 0)), constant_values=-1)
    frame_start = lax.axis_index("tm") * frame_count
    row_start = lax.axis_index("space") * row_count
    zero_index = jnp.int32(0)
    local_ids = lax.dynamic_slice(
        padded_ids,
        (frame_start, row_start, zero_index),
        (frame_count + 2, row_count + 2 * RT, window_table.shape[2]),
    )
    token_ids = jnp.repeat(local_ids, TILE, axis=2)
    block_frames = 4
    score_scale = 1.0 / math.sqrt(HD)

    def one_block(block_index):
        block_start = block_index * block_frames
        query_block = lax.dynamic_slice_in_dim(queries, block_start, block_frames, 0).reshape(
            -1, head_count, HD
        )
        pair_block = lax.dynamic_slice_in_dim(widened, block_start, block_frames + 2, 0).reshape(
            -1, 2, head_count, HD
        )
        query_ids = lax.dynamic_slice(
            token_ids,
            (block_start + 1, jnp.int32(RT), zero_index),
            (block_frames, row_count, col_count),
        ).reshape(-1)
        key_ids = lax.dynamic_slice_in_dim(token_ids, block_start, block_frames + 2, 0).reshape(-1)
        allowed = jnp.concatenate(
            [
                query_ids[:, None] == key_ids[None, :],
                jnp.broadcast_to(text_allowed[None, :], (query_ids.shape[0], text_total)),
            ],
            axis=1,
        )
        key_block = jnp.concatenate([pair_block[:, 0], text_pairs[:, 0]], axis=0)
        value_block = jnp.concatenate([pair_block[:, 1], text_pairs[:, 1]], axis=0)
        per_head = lax.map(
            lambda head_index: attend_head(
                query_block, key_block, value_block, allowed, score_scale, head_index
            ),
            jnp.arange(head_count, dtype=jnp.int32),
        )
        result = jnp.transpose(per_head, (1, 0, 2))
        return result.reshape(block_frames, row_count, col_count, feat_count)

    blocks = lax.map(one_block, jnp.arange(frame_count // block_frames, dtype=jnp.int32))
    return blocks.reshape(frame_count, row_count, col_count, feat_count)


def solution(mesh):
    in_specs = (
        P("tm", "space", None, "head"),
        P("tm", "space", None, "head"),
        P("tm", "space", None, "head"),
        P("tm", "head"),
        P("tm", "head"),
        P(),
        P(),
    )
    out_specs = P("tm", "space", None, "head")
    return jax.shard_map(
        per_device, mesh=mesh, in_specs=in_specs, out_specs=out_specs, check_vma=False
    )
```

profile of v0, /device:TPU:1, one launch (start us, length us, event | category | flops | bytes accessed | tf_op | source)
XLA Modules:
  0.0 318.9 jit_solution(13147145708185201784)
XLA Ops:
  0.0 1.6 constant_dynamic-update-slice_fusion.2
  2.1 6.2 %collective-permute-start = (bf16[1,4,32,1536]{3,2,1,0:T(8,128)(2,1)S(1)}, bf16[1,4,32,1536]{3,2,1,0:T(8,128)(2,1)S(1)}, u32[]{:S(2)}, u32[]{:S(2)}) collective-permute-start(bf16[1,4,32,1536]{3,2,1,0:T(8,128)(2,1)S(1)} %get-tuple-element.232), channel_id=1, source_target_pairs={{0,64},{64,128},{128,192},{1,65},{65,129},{129,193},{2,66},{66,130... | collective-permute-start | bytes 1179656 | tf_op jit(solution)/shard_map/ppermute | solution.py:18
  8.3 2.1 collective-permute-start.1
  10.4 2.6 collective-permute-done
  13.0 6.1 %collective-permute-done.1 = bf16[1,4,32,1536]{3,2,1,0:T(8,128)(2,1)S(1)} collective-permute-done((bf16[1,4,32,1536]{3,2,1,0:T(8,128)(2,1)S(1)}, bf16[1,4,32,1536]{3,2,1,0:T(8,128)(2,1)S(1)}, u32[]{:S(2)}, u32[]{:S(2)}) %collective-permute-start.1) | collective-permute-done | bytes 393248 | tf_op jit(solution)/shard_map/ppermute | solution.py:21
  19.1 2.1 pad_maximum_fusion.3
  21.2 5.4 %collective-permute-start.2 = (bf16[10,4,32,1536]{3,2,1,0:T(8,128)(2,1)}, bf16[10,4,32,1536]{3,2,1,0:T(8,128)(2,1)}, u32[]{:S(2)}, u32[]{:S(2)}) collective-permute-start(bf16[10,4,32,1536]{3,2,1,0:T(8,128)(2,1)} %pad_maximum_fusion.3), channel_id=1, source_target_pairs={{0,4},{4,8},{8,12},{12,16},{16,20},{20,24},{24,28},{28,32},{32,36}... | collective-permute-start | bytes 11796488 | tf_op jit(solution)/shard_map/ppermute | solution.py:18
  26.6 1.3 collective-permute-start.3
  28.2 82.2 %all_gather.3 = bf16[128,1536]{1,0:T(8,128)(2,1)} all-gather(bf16[32,1536]{1,0:T(8,128)(2,1)S(1)} %pad_maximum_fusion.4), channel_id=1, replica_groups=mesh['tm'=4,'space'=16,'head'=4] {'tm'}, dimensions={0}, use_global_device_ids=true | all-gather | bytes 491520 | tf_op jit(solution)/shard_map/all_gather | solution.py:49
  110.4 1.9 copy.22
  112.3 2.1 copy.23
  114.4 9.2 %pad_maximum_fusion.2 = bf16[10,12,32,1536]{3,2,1,0:T(8,128)(2,1)} fusion(bf16[10,4,32,1536]{3,2,1,0:T(8,128)(2,1)} %collective-permute-done.3, bf16[1,4,32,1536]{3,2,1,0:T(8,128)(2,1)} %copy-done.3, bf16[8,4,32,1536]{3,2,1,0:T(8,128)(2,1)S(1)} %constant_dynamic-update-slice_fusion.1, bf16[1,4,32,1536]{3,2,1,0:T(8,128)(2,1)} %copy-done.2, ...), kind=kLoop, calls=%fused_computation.34 | loop fusion | flops 23592960 | bytes 23592960 | tf_op jit(solution)/shard_map/concatenate | solution.py:22
  123.6 195.2 %while.34 = (s32[]{:T(128)}, bf16[2,4,4,32,768]{4,3,2,1,0:T(8,128)(2,1)}, s32[2]{0:T(128)S(1)}, bf16[8,4,32,768]{3,2,1,0:T(8,128)(2,1)}, bf16[10,12,32,1536]{3,2...) while((s32[]{:T(128)}, ...), condition=%wide.region_5.6_spmd.clone, body=%wide.region_0.5_spmd.clone.sunk | while | flops 652541056 | bytes 105521744 | solution.py:100
  124.8 6.8 %constant_dynamic-slice_fusion.9 = bf16[6,12,32,1536]{3,2,1,0:T(8,128)(2,1)} fusion(bf16[10,12,32,1536]{3,2,1,0:T(8,128)(2,1)} %get-tuple-element.429, s32[]{:T(128)S(6)} %select_n.47), kind=kLoop, calls=%fused_computation.31.clone.1 | loop fusion | bytes 14155780 | tf_op jit(solution)/shard_map/while/body/eval_jaxpr/dynamic_slice | solution.py:73
  131.6 15.1 %reshape.41 = bf16[2304,2,6,128]{3,2,1,0:T(8,128)(2,1)} reshape(bf16[6,12,32,1536]{3,2,1,0:T(8,128)(2,1)} %constant_dynamic-slice_fusion.9) | data formatting | bytes 14155776 | tf_op jit(solution)/shard_map/while/body/eval_jaxpr/reshape | solution.py:73
  146.7 4.4 %slice_bitcast_fusion.7 = (bf16[2304,6,128]{2,1,0:T(8,128)(2,1)S(1)}, bf16[2304,6,128]{2,1,0:T(8,128)(2,1)S(1)}) fusion(bf16[2304,2,6,128]{3,2,1,0:T(8,128)(2,1)} %reshape.41), kind=kLoop, calls=%fused_computation.23.clone.1 | loop fusion | bytes 14155776 | tf_op jit(solution)/shard_map/while/body/eval_jaxpr/squeeze | solution.py:90
  151.2 11.6 %pad_maximum_fusion.6 = (bf16[2432,6,128]{2,1,0:T(8,128)(2,1)S(1)}, bf16[2432,6,128]{2,1,0:T(8,128)(2,1)S(1)}) fusion(bf16[128,6,128]{2,1,0:T(8,128)(2,1)S(1)} %get-tuple-element.342, bf16[2304,6,128]{2,1,0:T(8,128)(2,1)S(1)} %get-tuple-element.343, bf16[128,6,128]{2,1,0:T(8,128)(2,1)S(1)} %get-tuple-element.344, ...), kind=kLoop, calls=%fused_computation.20.clone.1 | loop fusion | flops 3735552 | bytes 14942208 | tf_op jit(solution)/shard_map/while/body/eval_jaxpr/concatenate | solution.py:89
  162.9 2.4 copy.30
  165.2 2.3 copy.31
  169.8 1.2 constant_dynamic-slice_fusion.8
  171.0 0.9 reshape.40
  172.0 46.8 %while.35 = (s32[]{:T(128)}, bf16[6,512,128]{2,1,0:T(8,128)(2,1)S(1)}, s32[6]{0:T(128)S(1)}, bf16[512,6,128]{2,0,1:T(8,128)(2,1)S(1)}, bf16[2432,6,128]{2,0,1:T(...) while((s32[]{:T(128)}, ...), condition=%wide.region_4.4_spmd, body=%wide.region_1.3_spmd.sunk | while | flops 646380544 | bytes 17706648 | solution.py:91
  174.7 2.3 fusion.37
  177.0 0.8 fusion.38
  177.8 2.0 fusion.39
  182.5 2.3 fusion.37
  184.8 0.8 fusion.38
  185.6 2.0 fusion.39
  190.3 2.3 fusion.37
  192.6 0.8 fusion.38
  193.4 2.0 fusion.39
  198.1 2.3 fusion.37
  200.4 0.8 fusion.38
  201.2 2.0 fusion.39
  205.9 2.3 fusion.37
  208.2 0.8 fusion.38
  209.0 2.0 fusion.39
  213.7 2.3 fusion.37
  216.8 2.0 fusion.39
  219.4 0.9 broadcast_in_dim.39
  220.3 0.9 constant_dynamic-update-slice_fusion.4
  222.4 6.8 %constant_dynamic-slice_fusion.9 = bf16[6,12,32,1536]{3,2,1,0:T(8,128)(2,1)} fusion(bf16[10,12,32,1536]{3,2,1,0:T(8,128)(2,1)} %get-tuple-element.429, s32[]{:T(128)S(6)} %select_n.47), kind=kLoop, calls=%fused_computation.31.clone.1 | loop fusion | bytes 14155780 | tf_op jit(solution)/shard_map/while/body/eval_jaxpr/dynamic_slice | solution.py:73
  229.2 15.1 %reshape.41 = bf16[2304,2,6,128]{3,2,1,0:T(8,128)(2,1)} reshape(bf16[6,12,32,1536]{3,2,1,0:T(8,128)(2,1)} %constant_dynamic-slice_fusion.9) | data formatting | bytes 14155776 | tf_op jit(solution)/shard_map/while/body/eval_jaxpr/reshape | solution.py:73
  244.3 4.4 %slice_bitcast_fusion.7 = (bf16[2304,6,128]{2,1,0:T(8,128)(2,1)S(1)}, bf16[2304,6,128]{2,1,0:T(8,128)(2,1)S(1)}) fusion(bf16[2304,2,6,128]{3,2,1,0:T(8,128)(2,1)} %reshape.41), kind=kLoop, calls=%fused_computation.23.clone.1 | loop fusion | bytes 14155776 | tf_op jit(solution)/shard_map/while/body/eval_jaxpr/squeeze | solution.py:90
  248.8 11.6 %pad_maximum_fusion.6 = (bf16[2432,6,128]{2,1,0:T(8,128)(2,1)S(1)}, bf16[2432,6,128]{2,1,0:T(8,128)(2,1)S(1)}) fusion(bf16[128,6,128]{2,1,0:T(8,128)(2,1)S(1)} %get-tuple-element.342, bf16[2304,6,128]{2,1,0:T(8,128)(2,1)S(1)} %get-tuple-element.343, bf16[128,6,128]{2,1,0:T(8,128)(2,1)S(1)} %get-tuple-element.344, ...), kind=kLoop, calls=%fused_computation.20.clone.1 | loop fusion | flops 3735552 | bytes 14942208 | tf_op jit(solution)/shard_map/while/body/eval_jaxpr/concatenate | solution.py:89
  260.5 2.4 copy.30
  262.8 2.3 copy.31
  267.4 1.2 constant_dynamic-slice_fusion.8
  268.6 0.9 reshape.40
  269.6 46.8 %while.35 = (s32[]{:T(128)}, bf16[6,512,128]{2,1,0:T(8,128)(2,1)S(1)}, s32[6]{0:T(128)S(1)}, bf16[512,6,128]{2,0,1:T(8,128)(2,1)S(1)}, bf16[2432,6,128]{2,0,1:T(...) while((s32[]{:T(128)}, ...), condition=%wide.region_4.4_spmd, body=%wide.region_1.3_spmd.sunk | while | flops 646380544 | bytes 17706648 | solution.py:91
  272.3 2.3 fusion.37
  275.4 2.0 fusion.39
  280.1 2.3 fusion.37
  283.2 2.0 fusion.39
  287.9 2.3 fusion.37
  291.0 2.0 fusion.39
  295.7 2.3 fusion.37
  298.8 2.0 fusion.39
  303.5 2.3 fusion.37
  306.6 2.0 fusion.39
  311.4 2.3 fusion.37
  314.4 2.0 fusion.39
  317.0 0.9 broadcast_in_dim.39
  317.9 0.9 constant_dynamic-update-slice_fusion.4
  (73 shorter events, 21.2 us)
Async XLA Ops:
  0.0 1.9 copy-start.1
  2.1 10.9 %collective-permute-start = (bf16[1,4,32,1536]{3,2,1,0:T(8,128)(2,1)S(1)}, bf16[1,4,32,1536]{3,2,1,0:T(8,128)(2,1)S(1)}, u32[]{:S(2)}, u32[]{:S(2)}) collective-permute-start(bf16[1,4,32,1536]{3,2,1,0:T(8,128)(2,1)S(1)} %get-tuple-element.232), channel_id=1, source_target_pairs={{0,64},{64,128},{128,192},{1,65},{65,129},{129,193},{2,66},{66,130... | collective-permute-start | bytes 1179656 | tf_op jit(solution)/shard_map/ppermute | solution.py:18
  8.3 19.6 %copy-start.4 = (s32[32,64,4]{1,2,0:T(4,128)S(1)}, s32[32,64,4]{1,2,0:T(4,128)}, u32[]{:S(2)}) copy-start(s32[32,64,4]{1,2,0:T(4,128)} %param.17) | copy-start | bytes 98308
  8.3 19.9 %copy-start.5 = (bf16[32,768]{1,0:T(8,128)(2,1)S(1)}, bf16[32,768]{1,0:T(8,128)(2,1)}, u32[]{:S(2)}) copy-start(bf16[32,768]{1,0:T(8,128)(2,1)} %param.15) | copy-start | bytes 147460
  8.3 19.9 %copy-start.6 = (bf16[32,768]{1,0:T(8,128)(2,1)S(1)}, bf16[32,768]{1,0:T(8,128)(2,1)}, u32[]{:S(2)}) copy-start(bf16[32,768]{1,0:T(8,128)(2,1)} %param.14) | copy-start | bytes 147460
  8.3 10.7 %collective-permute-start.1 = (bf16[1,4,32,1536]{3,2,1,0:T(8,128)(2,1)S(1)}, bf16[1,4,32,1536]{3,2,1,0:T(8,128)(2,1)S(1)}, u32[]{:S(2)}, u32[]{:S(2)}) collective-permute-start(bf16[1,4,32,1536]{3,2,1,0:T(8,128)(2,1)S(1)} %get-tuple-element.233), channel_id=1, source_target_pairs={{64,0},{128,64},{192,128},{65,1},{129,65},{193,129},{66,2},{130,66... | collective-permute-start | bytes 1179656 | tf_op jit(solution)/shard_map/ppermute | solution.py:21
  13.0 8.2 %copy-start.2 = (bf16[1,4,32,1536]{3,2,1,0:T(8,128)(2,1)}, bf16[1,4,32,1536]{3,2,1,0:T(8,128)(2,1)S(1)}, u32[]{:S(2)}) copy-start(bf16[1,4,32,1536]{3,2,1,0:T(8,128)(2,1)S(1)} %collective-permute-done) | copy-start | bytes 1179652
  19.1 2.1 copy-start.3
  21.2 93.2 %collective-permute-start.2 = (bf16[10,4,32,1536]{3,2,1,0:T(8,128)(2,1)}, bf16[10,4,32,1536]{3,2,1,0:T(8,128)(2,1)}, u32[]{:S(2)}, u32[]{:S(2)}) collective-permute-start(bf16[10,4,32,1536]{3,2,1,0:T(8,128)(2,1)} %pad_maximum_fusion.3), channel_id=1, source_target_pairs={{0,4},{4,8},{8,12},{12,16},{16,20},{20,24},{24,28},{28,32},{32,36}... | collective-permute-start | bytes 11796488 | tf_op jit(solution)/shard_map/ppermute | solution.py:18
  26.6 87.8 %collective-permute-start.3 = (bf16[10,4,32,1536]{3,2,1,0:T(8,128)(2,1)}, bf16[10,4,32,1536]{3,2,1,0:T(8,128)(2,1)}, u32[]{:S(2)}, u32[]{:S(2)}) collective-permute-start(bf16[10,4,32,1536]{3,2,1,0:T(8,128)(2,1)} %pad_maximum_fusion.3), channel_id=1, source_target_pairs={{4,0},{8,4},{12,8},{16,12},{20,16},{24,20},{28,24},{32,28},{36,32}... | collective-permute-start | bytes 11796488 | tf_op jit(solution)/shard_map/ppermute | solution.py:21
  146.7 4.4 %copy-start = (bf16[128,2,6,128]{3,2,0,1:T(8,128)(2,1)S(1)}, bf16[128,2,6,128]{3,2,0,1:T(8,128)(2,1)}, u32[]{:S(2)}) copy-start(bf16[128,2,6,128]{3,2,0,1:T(8,128)(2,1)} %get-tuple-element.430) | copy-start | bytes 1179652 | tf_op jit(solution)/shard_map/while
  244.3 4.4 %copy-start = (bf16[128,2,6,128]{3,2,0,1:T(8,128)(2,1)S(1)}, bf16[128,2,6,128]{3,2,0,1:T(8,128)(2,1)}, u32[]{:S(2)}) copy-start(bf16[128,2,6,128]{3,2,0,1:T(8,128)(2,1)} %get-tuple-element.430) | copy-start | bytes 1179652 | tf_op jit(solution)/shard_map/while
where the time goes:
time: 322 us; the launch traced here: 319 us
  local copies, waits for them, and re-layouts  87 us (27%)
  blocking collectives  82.2 us (26%)
  matrix products  51.4 us (16%)
  other arithmetic  48.4 us (15%)
  loops' own time  26 us (8%)
  starting transfers between devices  15 us (5%)
  waiting for transfers between devices  8.67 us (3%)
    all_gather x1, blocking collectives, per_device(): lax.all_gather(jnp.concatenate([text_keys, text_values], axis=1), 'tm', a...  82.2 us
    reshape x2, local copies, waits for them, and re-layouts, one_block(): lax.dynamic_slice_in_dim(widened, block_start, block_frames + 2, 0)  30.3 us
    dot_general x12, matrix products, attend_head(): jnp.einsum('qd,kd->qk', query_one, key_one, preferred_element_type=jnp.fl...  27.4 us
    another operation x2, loops' own time, one_block(): lax.map(lambda head_index: attend_head(query_block, key_block, value_bloc...  24.6 us
    dot_general x12, matrix products, attend_head(): summed = jnp.dot(weights_low, value_one, preferred_element_type=jnp.float32)  24.1 us
    concatenate x2, other arithmetic, one_block(): key_block = jnp.concatenate([pair_block[:, 0], text_pairs[:, 0]], axis=0)  23.3 us
    dynamic_slice x2, local copies, waits for them, and re-layouts, one_block(): lax.dynamic_slice_in_dim(widened, block_start, block_frames + 2, 0)  13.6 us
    ppermute x2, starting transfers between devices, with_halo(): lax.ppermute(lax.slice_in_dim(block, block.shape[dim] - width, None, axis...  11.6 us
  transfers between devices with their start and end apart: 4, of which 2 were waited for; matrix products, arithmetic and copies ran while one was open for 1% of the time, Pallas kernels for 0%

commit v1 on v0

v1 whole, which is shorter than its diff:
```python
import functools
import math

import jax
import jax.numpy as jnp
from jax import lax
from jax.experimental import pallas as pl
from jax.experimental.pallas import tpu as pltpu
from jax.sharding import PartitionSpec as P

TILE = 8
HD = 128
MESH = pl.DeviceIdType.MESH
NT = (((1,), (1,)), ((), ()))


def kernel(
    tm_count,
    space_count,
    count_ref,
    table_ref,
    q_ref,
    k_ref,
    v_ref,
    text_k_ref,
    text_v_ref,
    out_ref,
    queries,
    keys,
    values,
    text_keys,
    text_values,
    result,
    ids,
    query_ids,
    weights_ref,
    denominators,
    z_send,
    z_recv,
    t_send,
    t_recv,
    text_send,
    text_recv,
    local_sem,
    out_sem,
):
    frames, rows, cols, feat = q_ref.shape
    heads = feat // HD
    tokens = rows * cols
    text_rows = text_k_ref.shape[0]
    text_total = text_keys.shape[0]
    t = lax.axis_index("tm")
    s = lax.axis_index("space")
    has_low, has_high = s > 0, s < space_count - 1
    has_before, has_after = t > 0, t < tm_count - 1
    low, high = lax.rem(s + space_count - 1, space_count), lax.rem(s + 1, space_count)
    before, after = lax.rem(t + tm_count - 1, tm_count), lax.rem(t + 1, tm_count)
    half = space_count // 2
    crosses_up, crosses_down = s == half - 1, s == half
    relays_up, relays_down = s == space_count - 1, s == 0
    is_middle = jnp.logical_or(crosses_up, crosses_down)
    is_outer = jnp.logical_or(relays_up, relays_down)
    sources = ((k_ref, keys), (v_ref, values))

    def both(*conditions):
        return functools.reduce(jnp.logical_and, conditions)

    def place_of(part):
        if isinstance(part, int) and part < 2:
            frame = 0 if part == 0 else frames - 1
            return (pl.ds(frame, 1),), (pl.ds(frame + 1, 1),)
        lanes = pl.ds(pl.multiple_of((part - 2) * HD, HD), HD)
        inner = (slice(None), slice(None), lanes)
        return (pl.ds(1, frames - 2), *inner), (pl.ds(2, frames - 2), *inner)

    def z_copy(up, which, part, kind=0):
        source, target = sources[which]
        slot = 0 if up else 2
        side = slot // 2
        here, there = place_of(part)
        if kind == 0:
            peer = high if up else low
        elif kind == 1:
            peer = space_count - 1 if up else 0
        else:
            peer = half if up else half - 1
        src = target.at[(2 - slot, *there)] if kind == 2 else source.at[here]
        dst = target.at[(2 - slot if kind == 1 else slot, *there)]
        return pltpu.make_async_remote_copy(
            src_ref=src,
            dst_ref=dst,
            send_sem=z_send.at[side, which, part],
            recv_sem=z_recv.at[1 - side if kind == 1 else side, which, part],
            device_id={"space": peer},
            device_id_type=MESH,
        )

    def t_copy(forward, which, slot):
        source, target = sources[which]
        peer = after if forward else before
        frame = frames - 1 if forward else 0
        place = 0 if forward else frames + 1
        if slot == 1:
            src = source.at[pl.ds(frame, 1)]
        else:
            src = target.at[slot, pl.ds(frame + 1, 1)]
        side = 0 if forward else 1
        return pltpu.make_async_remote_copy(
            src_ref=src,
            dst_ref=target.at[slot, pl.ds(place, 1)],
            send_sem=t_send.at[side, which, slot],
            recv_sem=t_recv.at[side, which, slot],
            device_id={"tm": peer},
            device_id_type=MESH,
        )

    own_rows = pl.ds(pl.multiple_of(t * text_rows, text_rows), text_rows)

    def text_copy(step, which):
        src, target = ((text_k_ref, text_keys), (text_v_ref, text_values))[which]
        return pltpu.make_async_remote_copy(
            src_ref=src,
            dst_ref=target.at[own_rows],
            send_sem=text_send.at[step, which],
            recv_sem=text_recv.at[step, which],
            device_id={"tm": lax.rem(t + step, tm_count)},
            device_id_type=MESH,
        )

    local_copies = [
        pltpu.make_async_copy(q_ref, queries, local_sem.at[0]),
        pltpu.make_async_copy(k_ref, keys.at[1, pl.ds(1, frames)], local_sem.at[1]),
        pltpu.make_async_copy(v_ref, values.at[1, pl.ds(1, frames)], local_sem.at[2]),
        pltpu.make_async_copy(text_k_ref, text_keys.at[own_rows], local_sem.at[3]),
        pltpu.make_async_copy(text_v_ref, text_values.at[own_rows], local_sem.at[4]),
    ]

    barrier = pltpu.get_barrier_semaphore()

    def greet(where):
        pl.semaphore_signal(barrier, inc=1, device_id=where, device_id_type=MESH)

    pl.when(has_low)(lambda: greet({"space": low}))
    pl.when(has_high)(lambda: greet({"space": high}))

    @pl.when(is_middle)
    def _():
        greet({"space": 0})
        greet({"space": space_count - 1})

    @pl.when(is_outer)
    def _():
        greet({"space": half - 1})
        greet({"space": half})

    for step in range(1, tm_count):
        greet({"tm": lax.rem(t + step, tm_count)})
    pl.semaphore_wait(
        barrier,
        has_low.astype(jnp.int32)
        + has_high.astype(jnp.int32)
        + 2 * is_middle.astype(jnp.int32)
        + 2 * is_outer.astype(jnp.int32)
        + (tm_count - 1),
    )

    ways = (
        (True, has_high, crosses_up, relays_up, has_low),
        (False, has_low, crosses_down, relays_down, has_high),
    )

    def relayed(part):
        return part == 1 or part % 2 == 0 and part >= 2

    def start_part(part, through):
        for which in range(2):
            for up, sends, crosses, _, _ in ways:
                if through:
                    straight = both(sends, jnp.logical_not(crosses))
                    pl.when(straight)(z_copy(up, which, part).start)
                    pl.when(crosses)(z_copy(up, which, part, 1).start)
                else:
                    pl.when(sends)(z_copy(up, which, part).start)

    start_part(0, False)
    start_part(1, True)
    for which in range(2):
        pl.when(has_after)(t_copy(True, which, 1).start)
        pl.when(has_before)(t_copy(False, which, 1).start)
    for step in range(1, tm_count):
        for which in range(2):
            text_copy(step, which).start()

    @pl.loop(0, heads // 2)
    def _(pair):
        part = 2 * pair + 2
        start_part(part, True)
        for which in range(2):
            for up, sends, crosses, _, _ in ways:
                now = both(sends, jnp.logical_or(jnp.logical_not(crosses), pair == 0))
                pl.when(now)(z_copy(up, which, part + 1).start)

    for copy in local_copies:
        copy.start()

    blank = jnp.zeros((rows, cols, feat), values.dtype)
    short = jnp.zeros((rows, cols, HD), values.dtype)

    def clear_group(slot):
        for frame in (0, 1, frames + 1):
            values[slot, frame] = blank

        @pl.loop(2, frames)
        def _(frame):
            for head in range(1, heads, 2):
                values[slot, frame, :, :, head * HD : (head + 1) * HD] = short

    def clear_frame(frame):
        for slot in range(3):
            values[slot, frame] = blank

    pl.when(relays_down)(lambda: clear_group(0))
    pl.when(relays_up)(lambda: clear_group(2))
    pl.when(jnp.logical_not(has_before))(lambda: clear_frame(0))
    pl.when(jnp.logical_not(has_after))(lambda: clear_frame(frames + 1))

    tile_count = table_ref.shape[1]
    row_total = table_ref.shape[2]
    frame_total = table_ref.shape[0]
    span = 3 * tokens
    row_at = lax.broadcasted_iota(jnp.int32, (row_total, span), 0)
    lane_at = lax.broadcasted_iota(jnp.int32, (row_total, span), 1)
    row_hit = row_at == s * rows - rows + lane_at // cols
    tile_at = (lane_at // TILE) % tile_count
    high_part = jnp.zeros((frame_total, span), jnp.float32)
    low_part = jnp.zeros((frame_total, span), jnp.float32)
    for tile in range(tile_count):
        pick = jnp.logical_and(row_hit, tile_at == tile).astype(jnp.float32).astype(jnp.bfloat16)
        column = table_ref[:, tile, :]
        for_high = (column // 128).astype(jnp.float32).astype(jnp.bfloat16)
        for_low = (column % 128).astype(jnp.float32).astype(jnp.bfloat16)
        high_part += jnp.dot(for_high, pick, preferred_element_type=jnp.float32)
        low_part += jnp.dot(for_low, pick, preferred_element_type=jnp.float32)
    near_frames = frames + 2
    frame_at = lax.broadcasted_iota(jnp.int32, (2 * frames, frame_total), 1)
    wanted = lax.broadcasted_iota(jnp.int32, (2 * frames, frame_total), 0) + t * frames - 1
    pick = (frame_at == wanted).astype(jnp.float32).astype(jnp.bfloat16)
    near_high = jnp.dot(pick, high_part.astype(jnp.bfloat16), preferred_element_type=jnp.float32)
    near_low = jnp.dot(pick, low_part.astype(jnp.bfloat16), preferred_element_type=jnp.float32)
    near_ids = near_high * 128.0 + near_low
    for frame in range(near_frames):
        ids[frame] = jnp.broadcast_to(near_ids[frame : frame + 1, :], (8, span))

    @pl.loop(0, frames)
    def _(frame):
        row = ids[frame + 1, 0:1, tokens : 2 * tokens]
        query_ids[frame] = jnp.transpose(jnp.broadcast_to(row, (tokens, tokens)))

    def pass_on(part, which):
        for up, _, _, relays, _ in ways:

            @pl.when(relays)
            def _(up=up):
                z_copy(up, which, part, 1).wait_recv()
                z_copy(up, which, part, 2).start()

    for which in range(2):
        pass_on(1, which)
    for part in range(2):
        forward = part == 1
        goes = has_after if forward else has_before
        for which in range(2):
            for up, _, _, _, receives in ways:

                @pl.when(receives)
                def _(up=up, which=which, part=part, forward=forward, goes=goes):
                    z_copy(up, which, part).wait_recv()
                    pl.when(goes)(t_copy(forward, which, 0 if up else 2).start)

    for copy in local_copies:
        copy.wait()

    def wait_halo(which):
        for step in range(1, tm_count):
            text_copy(step, which).wait_recv()
        for slot, there in ((1, None), (0, has_low), (2, has_high)):
            for forward, comes in ((True, has_before), (False, has_after)):
                arrives = comes if there is None else both(comes, there)
                pl.when(arrives)(t_copy(forward, which, slot).wait_recv)

    scale = math.log2(math.e) / math.sqrt(HD)
    text_allowed = lax.broadcasted_iota(jnp.int32, (tokens, text_total), 1) < count_ref[0]

    def out_copy(head):
        lanes = pl.ds(pl.multiple_of(head * HD, HD), HD)
        return pltpu.make_async_copy(
            result.at[:, :, :, lanes], out_ref.at[:, :, :, lanes], out_sem.at[head]
        )

    @pl.loop(0, heads)
    def _(head):
        lanes = pl.ds(pl.multiple_of(head * HD, HD), HD)

        @pl.when(head < heads // 2)
        def _():
            for which in range(2):
                pass_on(2 * head + 2, which)

        @pl.when(head == 0)
        def _():
            wait_halo(0)

        for up, _, _, _, receives in ways:
            pl.when(receives)(z_copy(up, 0, head + 2).wait_recv)

        later = both(lax.rem(head, 2) == 0, head < heads - 2)
        for which in range(2):
            for up, _, crosses, _, _ in ways:
                pl.when(both(crosses, later))(z_copy(up, which, head + 5).start)

        @pl.loop(0, frames)
        def _(frame):
            query = queries[frame, :, :, lanes].reshape(tokens, HD)
            own = query_ids[frame]
            near = pl.ds(frame, 3)
            scores = []
            for slot in range(3):
                key = keys[slot, near, :, :, lanes].reshape(3 * tokens, HD)
                raw = lax.dot_general(query, key, NT, preferred_element_type=jnp.float32)
                for j in range(3):
                    there = ids[frame + j, 0:1, slot * tokens : (slot + 1) * tokens]
                    piece = raw[:, j * tokens : (j + 1) * tokens]
                    scores.append(jnp.where(own == there, piece, -jnp.inf))
            raw = lax.dot_general(
                query, text_keys[:, lanes], NT, preferred_element_type=jnp.float32
            )
            scores.append(jnp.where(text_allowed, raw, -jnp.inf))
            highest = jnp.max(functools.reduce(jnp.maximum, scores), axis=1, keepdims=True)
            weights = [jnp.exp2((score - highest) * scale) for score in scores]
            denominator = jnp.sum(functools.reduce(jnp.add, weights), axis=1, keepdims=True)
            denominators[frame] = jnp.broadcast_to(denominator, (tokens, HD))
            for j, weight in enumerate(weights):
                weights_ref[frame, :, j * tokens : j * tokens + weight.shape[1]] = weight.astype(
                    jnp.bfloat16
                )

        @pl.when(head == 0)
        def _():
            wait_halo(1)

        for up, _, _, _, receives in ways:
            pl.when(receives)(z_copy(up, 1, head + 2).wait_recv)

        @pl.loop(0, frames)
        def _(frame):
            near = pl.ds(frame, 3)
            total = jnp.dot(
                weights_ref[frame, :, 9 * tokens :],
                text_values[:, lanes],
                preferred_element_type=jnp.float32,
            )
            for slot in range(3):
                value = values[slot, near, :, :, lanes].reshape(3 * tokens, HD)
                weight = weights_ref[frame, :, 3 * slot * tokens : 3 * (slot + 1) * tokens]
                total += jnp.dot(weight, value, preferred_element_type=jnp.float32)
            attended = (total / denominators[frame]).astype(jnp.bfloat16)
            result[frame, :, :, lanes] = attended.reshape(rows, cols, HD)

        out_copy(head).start()

    for part in range(heads + 2):
        for which in range(2):
            for up, sends, _, relays, _ in ways:
                out = jnp.logical_or(sends, relays) if relayed(part) else sends
                pl.when(out)(z_copy(up, which, part).wait_send)
    for slot, there in ((1, None), (0, has_low), (2, has_high)):
        for which in range(2):
            for forward, goes in ((True, has_after), (False, has_before)):
                leaves = goes if there is None else both(goes, there)
                pl.when(leaves)(t_copy(forward, which, slot).wait_send)
    for step in range(1, tm_count):
        for which in range(2):
            text_copy(step, which).wait_send()

    @pl.loop(0, heads)
    def _(head):
        out_copy(head).wait()


def per_device(
    tm_count,
    space_count,
    queries,
    key_rows,
    value_rows,
    text_keys,
    text_values,
    text_count,
    window_table,
):
    frames, rows, cols, feat = queries.shape
    heads = feat // HD
    tokens = rows * cols
    text_total = text_keys.shape[0] * tm_count
    table = jnp.transpose(window_table, (0, 2, 1))
    block = (3, frames + 2, rows, cols, feat)
    anywhere = pl.BlockSpec(memory_space=pl.ANY)
    key_total = 9 * tokens + text_total
    flops = 4 * frames * tokens * key_total * feat
    return pl.pallas_call(
        functools.partial(kernel, tm_count, space_count),
        out_shape=jax.ShapeDtypeStruct(queries.shape, queries.dtype),
        in_specs=[
            pl.BlockSpec(memory_space=pltpu.SMEM),
            pl.BlockSpec(memory_space=pltpu.VMEM),
        ]
        + [anywhere] * 5,
        out_specs=anywhere,
        scratch_shapes=[
            pltpu.VMEM(queries.shape, queries.dtype),
            pltpu.VMEM(block, key_rows.dtype),
            pltpu.VMEM(block, value_rows.dtype),
            pltpu.VMEM((text_total, feat), text_keys.dtype),
            pltpu.VMEM((text_total, feat), text_values.dtype),
            pltpu.VMEM(queries.shape, queries.dtype),
            pltpu.VMEM((frames + 2, 8, 3 * tokens), jnp.float32),
            pltpu.VMEM((frames, tokens, tokens), jnp.float32),
            pltpu.VMEM((frames, tokens, key_total), jnp.bfloat16),
            pltpu.VMEM((frames, tokens, HD), jnp.float32),
            pltpu.SemaphoreType.DMA((2, 2, heads + 2)),
            pltpu.SemaphoreType.DMA((2, 2, heads + 2)),
            pltpu.SemaphoreType.DMA((2, 2, 3)),
            pltpu.SemaphoreType.DMA((2, 2, 3)),
            pltpu.SemaphoreType.DMA((tm_count, 2)),
            pltpu.SemaphoreType.DMA((tm_count, 2)),
            pltpu.SemaphoreType.DMA((5,)),
            pltpu.SemaphoreType.DMA((heads,)),
        ],
        compiler_params=pltpu.CompilerParams(
            collective_id=0, has_side_effects=True, vmem_limit_bytes=56 * 2**20
        ),
        cost_estimate=pl.CostEstimate(
            flops=flops, bytes_accessed=4 * queries.size * 2, transcendentals=0
        ),
    )(text_count, table, queries, key_rows, value_rows, text_keys, text_values)


def solution(mesh):
    in_specs = (
        P("tm", "space", None, "head"),
        P("tm", "space", None, "head"),
        P("tm", "space", None, "head"),
        P("tm", "head"),
        P("tm", "head"),
        P(),
        P(),
    )
    out_specs = P("tm", "space", None, "head")
    return jax.shard_map(
        functools.partial(per_device, mesh.shape["tm"], mesh.shape["space"]),
        mesh=mesh,
        in_specs=in_specs,
        out_specs=out_specs,
        check_vma=False,
    )
```

time: 322 us -> 101 us (0.31)
  the two profiles are of different devices: /device:TPU:1 before, /device:TPU:15 now
where the time goes in v1:
time: 101 us; the launch traced here: 100 us
  Pallas kernels  97.1 us (96%)
  local copies, waits for them, and re-layouts  2.65 us (3%)
    pallas_call x1, Pallas kernels, per_device(): pl.pallas_call(functools.partial(kernel, tm_count, space_count), out_shap...  97.1 us
    unnamed x1, local copies, waits for them, and re-layouts  2.65 us

profile of v1, /device:TPU:15, one launch (start us, length us, event | category | flops | bytes accessed | tf_op | source)
XLA Modules:
  0.0 100.4 jit_solution(2124300703691739883)
XLA Ops:
  0.7 97.1 %shard_map.73 = bf16[8,4,32,768]{3,2,1,0:T(8,128)(2,1)} custom-call(s32[1]{0:T(128)S(6)} %copy.9.count_ref, s32[32,4,64]{2,1,0:T(4,128)} %bitcast.1, bf16[8,4,32,768]{3,2,1,0:T(8,128)(2,1)} %q_ref.1, bf16[8,4,32,768]{3,2,1,0:T(8,128)(2,1)} %k_ref.1, bf16[8,4,32,768]{3,2,1,0:T(8,128)(2,1)} %v_ref.1, bf16[32,768]{1,0:T(8,128)(2,1)} %text_k_ref.1, ...), custom_call_target="tpu_custom_call" | custom-call | flops 4026531840 | bytes 6291456 | tf_op jit(solution)/shard_map/pallas_call | solution.py:410
  97.8 2.7 %copy.10 = bf16[8,4,32,768]{3,2,1,0:T(8,128)(2,1)} copy(bf16[8,4,32,768]{3,2,1,0:T(8,128)(2,1)} %shard_map.73) | data formatting | bytes 3145728

commit v2 on v1

--- a/solution.py
+++ b/solution.py
@@ -30,7 +30,8 @@
     values,
     text_keys,
     text_values,
-    result,
+    count,
+    table,
     ids,
     query_ids,
     weights_ref,
@@ -42,7 +43,6 @@
     text_send,
     text_recv,
     local_sem,
-    out_sem,
 ):
     frames, rows, cols, feat = q_ref.shape
     heads = feat // HD
@@ -127,6 +127,10 @@
             device_id_type=MESH,
         )
 
+    first_copies = [
+        pltpu.make_async_copy(count_ref, count, local_sem.at[5]),
+        pltpu.make_async_copy(table_ref, table, local_sem.at[6]),
+    ]
     local_copies = [
         pltpu.make_async_copy(q_ref, queries, local_sem.at[0]),
         pltpu.make_async_copy(k_ref, keys.at[1, pl.ds(1, frames)], local_sem.at[1]),
@@ -136,6 +140,9 @@
     ]
 
     barrier = pltpu.get_barrier_semaphore()
+
+    for copy in first_copies:
+        copy.start()
 
     def greet(where):
         pl.semaphore_signal(barrier, inc=1, device_id=where, device_id_type=MESH)
@@ -224,9 +231,9 @@
     pl.when(jnp.logical_not(has_before))(lambda: clear_frame(0))
     pl.when(jnp.logical_not(has_after))(lambda: clear_frame(frames + 1))
 
-    tile_count = table_ref.shape[1]
-    row_total = table_ref.shape[2]
-    frame_total = table_ref.shape[0]
+    for copy in first_copies:
+        copy.wait()
+    frame_total, tile_count, row_total = table.shape
     span = 3 * tokens
     row_at = lax.broadcasted_iota(jnp.int32, (row_total, span), 0)
     lane_at = lax.broadcasted_iota(jnp.int32, (row_total, span), 1)
@@ -236,7 +243,7 @@
     low_part = jnp.zeros((frame_total, span), jnp.float32)
     for tile in range(tile_count):
         pick = jnp.logical_and(row_hit, tile_at == tile).astype(jnp.float32).astype(jnp.bfloat16)
-        column = table_ref[:, tile, :]
+        column = table[:, tile, :]
         for_high = (column // 128).astype(jnp.float32).astype(jnp.bfloat16)
         for_low = (column % 128).astype(jnp.float32).astype(jnp.bfloat16)
         high_part += jnp.dot(for_high, pick, preferred_element_type=jnp.float32)
@@ -289,13 +296,7 @@
                 pl.when(arrives)(t_copy(forward, which, slot).wait_recv)
 
     scale = math.log2(math.e) / math.sqrt(HD)
-    text_allowed = lax.broadcasted_iota(jnp.int32, (tokens, text_total), 1) < count_ref[0]
-
-    def out_copy(head):
-        lanes = pl.ds(pl.multiple_of(head * HD, HD), HD)
-        return pltpu.make_async_copy(
-            result.at[:, :, :, lanes], out_ref.at[:, :, :, lanes], out_sem.at[head]
-        )
+    text_allowed = lax.broadcasted_iota(jnp.int32, (tokens, text_total), 1) < count[0]
 
     @pl.loop(0, heads)
     def _(head):
@@ -318,7 +319,7 @@
             for up, _, crosses, _, _ in ways:
                 pl.when(both(crosses, later))(z_copy(up, which, head + 5).start)
 
-        @pl.loop(0, frames)
+        @pl.loop(0, frames, unroll=True)
         def _(frame):
             query = queries[frame, :, :, lanes].reshape(tokens, HD)
             own = query_ids[frame]
@@ -351,7 +352,7 @@
         for up, _, _, _, receives in ways:
             pl.when(receives)(z_copy(up, 1, head + 2).wait_recv)
 
-        @pl.loop(0, frames)
+        @pl.loop(0, frames, unroll=True)
         def _(frame):
             near = pl.ds(frame, 3)
             total = jnp.dot(
@@ -364,9 +365,7 @@
                 weight = weights_ref[frame, :, 3 * slot * tokens : 3 * (slot + 1) * tokens]
                 total += jnp.dot(weight, value, preferred_element_type=jnp.float32)
             attended = (total / denominators[frame]).astype(jnp.bfloat16)
-            result[frame, :, :, lanes] = attended.reshape(rows, cols, HD)
-
-        out_copy(head).start()
+            out_ref[frame, :, :, lanes] = attended.reshape(rows, cols, HD)
 
     for part in range(heads + 2):
         for which in range(2):
@@ -381,10 +380,6 @@
     for step in range(1, tm_count):
         for which in range(2):
             text_copy(step, which).wait_send()
-
-    @pl.loop(0, heads)
-    def _(head):
-        out_copy(head).wait()
 
 
 def per_device(
@@ -409,20 +404,17 @@
     flops = 4 * frames * tokens * key_total * feat
     return pl.pallas_call(
         functools.partial(kernel, tm_count, space_count),
-        out_shape=jax.ShapeDtypeStruct(queries.shape, queries.dtype),
-        in_specs=[
-            pl.BlockSpec(memory_space=pltpu.SMEM),
-            pl.BlockSpec(memory_space=pltpu.VMEM),
-        ]
-        + [anywhere] * 5,
-        out_specs=anywhere,
+        out_shape=pltpu.VMEM(queries.shape, queries.dtype),
+        in_specs=[anywhere] * 7,
+        out_specs=pl.BlockSpec(memory_space=pltpu.VMEM),
         scratch_shapes=[
             pltpu.VMEM(queries.shape, queries.dtype),
             pltpu.VMEM(block, key_rows.dtype),
             pltpu.VMEM(block, value_rows.dtype),
             pltpu.VMEM((text_total, feat), text_keys.dtype),
             pltpu.VMEM((text_total, feat), text_values.dtype),
-            pltpu.VMEM(queries.shape, queries.dtype),
+            pltpu.SMEM(text_count.shape, text_count.dtype),
+            pltpu.VMEM(table.shape, table.dtype),
             pltpu.VMEM((frames + 2, 8, 3 * tokens), jnp.float32),
             pltpu.VMEM((frames, tokens, tokens), jnp.float32),
             pltpu.VMEM((frames, tokens, key_total), jnp.bfloat16),
@@ -433,8 +425,7 @@
             pltpu.SemaphoreType.DMA((2, 2, 3)),
             pltpu.SemaphoreType.DMA((tm_count, 2)),
             pltpu.SemaphoreType.DMA((tm_count, 2)),
-            pltpu.SemaphoreType.DMA((5,)),
-            pltpu.SemaphoreType.DMA((heads,)),
+            pltpu.SemaphoreType.DMA((7,)),
         ],
         compiler_params=pltpu.CompilerParams(
             collective_id=0, has_side_effects=True, vmem_limit_bytes=56 * 2**20

time: 101 us -> 79.5 us (0.79)
  Pallas kernels: 97.1 us -> 77.7 us
  local copies, waits for them, and re-layouts: 2.65 us -> 1.15 us
    pallas_call x1, Pallas kernels: 97.1 us -> 77.7 us  [per_device(): pl.pallas_call(functools.partial(kernel, tm_count, space_count), out_shap...]
    unnamed x1, local copies, waits for them, and re-layouts: 2.65 us -> 1.15 us
where the time goes in v2:
time: 79.5 us
  Pallas kernels  77.7 us (98%)
  local copies, waits for them, and re-layouts  1.15 us (1%)
    pallas_call x1, Pallas kernels, per_device(): pl.pallas_call(functools.partial(kernel, tm_count, space_count), out_shap...  77.7 us

profile of v2, /device:TPU:15, one launch (start us, length us, event | category | flops | bytes accessed | tf_op | source)
XLA Modules:
  0.0 79.5 jit_solution(14807868182311858117)
XLA Ops:
  0.7 77.7 %shard_map.73 = bf16[8,4,32,768]{3,2,1,0:T(8,128)(2,1)S(1)} custom-call(s32[1]{0:T(128)S(6)} %copy.10.count_ref, s32[32,4,64]{2,1,0:T(4,128)} %bitcast.1, bf16[8,4,32,768]{3,2,1,0:T(8,128)(2,1)} %q_ref.1, bf16[8,4,32,768]{3,2,1,0:T(8,128)(2,1)} %k_ref.1, bf16[8,4,32,768]{3,2,1,0:T(8,128)(2,1)} %v_ref.1, bf16[32,768]{1,0:T(8,128)(2,1)} %text_k_ref.1, ...), custom_call_target="tpu_custom_call" | custom-call | flops 4026531840 | bytes 6291456 | tf_op jit(solution)/shard_map/pallas_call | solution.py:405
  78.3 1.1 %copy.9 = bf16[8,4,32,768]{3,2,1,0:T(8,128)(2,1)} copy(bf16[8,4,32,768]{3,2,1,0:T(8,128)(2,1)S(1)} %shard_map.73) | data formatting | bytes 3145728

commit v3 on v2

--- a/solution.py
+++ b/solution.py
@@ -65,19 +65,27 @@
     def both(*conditions):
         return functools.reduce(jnp.logical_and, conditions)
 
-    def place_of(part):
+    last, rest = heads + 1, heads + 2
+
+    def place_of(which, part):
         if isinstance(part, int) and part < 2:
             frame = 0 if part == 0 else frames - 1
             return (pl.ds(frame, 1),), (pl.ds(frame + 1, 1),)
-        lanes = pl.ds(pl.multiple_of((part - 2) * HD, HD), HD)
+        start, size, head = 1, frames - 2, part - 2
+        if isinstance(part, int) and which == 1:
+            if part == last:
+                size = frames - 3
+            elif part == rest:
+                start, size, head = frames - 2, 1, heads - 1
+        lanes = pl.ds(pl.multiple_of(head * HD, HD), HD)
         inner = (slice(None), slice(None), lanes)
-        return (pl.ds(1, frames - 2), *inner), (pl.ds(2, frames - 2), *inner)
+        return (pl.ds(start, size), *inner), (pl.ds(start + 1, size), *inner)
 
     def z_copy(up, which, part, kind=0):
         source, target = sources[which]
         slot = 0 if up else 2
         side = slot // 2
-        here, there = place_of(part)
+        here, there = place_of(which, part)
         if kind == 0:
             peer = high if up else low
         elif kind == 1:
@@ -114,18 +122,38 @@
             device_id_type=MESH,
         )
 
+    def passes_corner(forward, slot):
+        goes = has_after if forward else has_before
+        return goes if slot == 1 else both(goes, has_low if slot == 0 else has_high)
+
     own_rows = pl.ds(pl.multiple_of(t * text_rows, text_rows), text_rows)
 
-    def text_copy(step, which):
+    def text_copy(forward, which, hop):
         src, target = ((text_k_ref, text_keys), (text_v_ref, text_values))[which]
+        slab = lax.rem(t + (tm_count - hop if forward else hop), tm_count)
+        place = pl.ds(pl.multiple_of(slab * text_rows, text_rows), text_rows)
+        side = 0 if forward else 1
         return pltpu.make_async_remote_copy(
-            src_ref=src,
-            dst_ref=target.at[own_rows],
-            send_sem=text_send.at[step, which],
-            recv_sem=text_recv.at[step, which],
-            device_id={"tm": lax.rem(t + step, tm_count)},
+            src_ref=src if hop == 0 else target.at[place],
+            dst_ref=target.at[place],
+            send_sem=text_send.at[side, which, hop],
+            recv_sem=text_recv.at[side, which, hop],
+            device_id={"tm": after if forward else before},
             device_id_type=MESH,
         )
+
+    def text_ways(hop):
+        return (
+            (True, t >= hop, both(t >= hop, has_after)),
+            (False, t < tm_count - hop, both(t < tm_count - hop, has_before)),
+        )
+
+    def text_hop(which, hop):
+        for forward, comes, goes in text_ways(hop):
+            if hop > 0:
+                pl.when(comes)(text_copy(forward, which, hop - 1).wait_recv)
+            if hop < tm_count - 1:
+                pl.when(goes)(text_copy(forward, which, hop).start)
 
     first_copies = [
         pltpu.make_async_copy(count_ref, count, local_sem.at[5]),
@@ -160,15 +188,16 @@
         greet({"space": half - 1})
         greet({"space": half})
 
-    for step in range(1, tm_count):
-        greet({"tm": lax.rem(t + step, tm_count)})
+    pl.when(has_before)(lambda: greet({"tm": before}))
+    pl.when(has_after)(lambda: greet({"tm": after}))
     pl.semaphore_wait(
         barrier,
         has_low.astype(jnp.int32)
         + has_high.astype(jnp.int32)
         + 2 * is_middle.astype(jnp.int32)
         + 2 * is_outer.astype(jnp.int32)
-        + (tm_count - 1),
+        + has_before.astype(jnp.int32)
+        + has_after.astype(jnp.int32),
     )
 
     ways = (
@@ -177,7 +206,7 @@
     )
 
     def relayed(part):
-        return part == 1 or part % 2 == 0 and part >= 2
+        return part % 2 == 0 and part >= 2
 
     def start_part(part, through):
         for which in range(2):
@@ -189,32 +218,35 @@
                 else:
                     pl.when(sends)(z_copy(up, which, part).start)
 
+    for which in range(2):
+        text_hop(which, 0)
     start_part(0, False)
-    start_part(1, True)
+    start_part(1, False)
     for which in range(2):
         pl.when(has_after)(t_copy(True, which, 1).start)
         pl.when(has_before)(t_copy(False, which, 1).start)
-    for step in range(1, tm_count):
-        for which in range(2):
-            text_copy(step, which).start()
-
-    @pl.loop(0, heads // 2)
-    def _(pair):
-        part = 2 * pair + 2
+
+    for part in range(2, heads + 2, 2):
         start_part(part, True)
         for which in range(2):
             for up, sends, crosses, _, _ in ways:
-                now = both(sends, jnp.logical_or(jnp.logical_not(crosses), pair == 0))
+                now = sends if part == 2 else both(sends, jnp.logical_not(crosses))
                 pl.when(now)(z_copy(up, which, part + 1).start)
+    for up, sends, crosses, _, _ in ways:
+        pl.when(both(sends, jnp.logical_not(crosses)))(z_copy(up, 1, rest).start)
 
     for copy in local_copies:
         copy.start()
 
+    for hop in range(1, tm_count):
+        for which in range(2):
+            text_hop(which, hop)
+
     blank = jnp.zeros((rows, cols, feat), values.dtype)
     short = jnp.zeros((rows, cols, HD), values.dtype)
 
     def clear_group(slot):
-        for frame in (0, 1, frames + 1):
+        for frame in (0, 1, frames, frames + 1):
             values[slot, frame] = blank
 
         @pl.loop(2, frames)
@@ -271,25 +303,18 @@
                 z_copy(up, which, part, 1).wait_recv()
                 z_copy(up, which, part, 2).start()
 
-    for which in range(2):
-        pass_on(1, which)
     for part in range(2):
         forward = part == 1
-        goes = has_after if forward else has_before
         for which in range(2):
             for up, _, _, _, receives in ways:
-
-                @pl.when(receives)
-                def _(up=up, which=which, part=part, forward=forward, goes=goes):
-                    z_copy(up, which, part).wait_recv()
-                    pl.when(goes)(t_copy(forward, which, 0 if up else 2).start)
+                slot = 0 if up else 2
+                pl.when(receives)(z_copy(up, which, part).wait_recv)
+                pl.when(passes_corner(forward, slot))(t_copy(forward, which, slot).start)
 
     for copy in local_copies:
         copy.wait()
 
     def wait_halo(which):
-        for step in range(1, tm_count):
-            text_copy(step, which).wait_recv()
         for slot, there in ((1, None), (0, has_low), (2, has_high)):
             for forward, comes in ((True, has_before), (False, has_after)):
                 arrives = comes if there is None else both(comes, there)
@@ -307,17 +332,19 @@
             for which in range(2):
                 pass_on(2 * head + 2, which)
 
+        for up, _, _, _, receives in ways:
+            pl.when(receives)(z_copy(up, 0, head + 2).wait_recv)
+
+        for now in range(0, heads - 2, 2):
+            for which in range(2):
+                for up, _, crosses, _, _ in ways:
+                    pl.when(both(crosses, head == now))(z_copy(up, which, now + 5).start)
+        for up, _, crosses, _, _ in ways:
+            pl.when(both(crosses, head == heads - 4))(z_copy(up, 1, rest).start)
+
         @pl.when(head == 0)
         def _():
             wait_halo(0)
-
-        for up, _, _, _, receives in ways:
-            pl.when(receives)(z_copy(up, 0, head + 2).wait_recv)
-
-        later = both(lax.rem(head, 2) == 0, head < heads - 2)
-        for which in range(2):
-            for up, _, crosses, _, _ in ways:
-                pl.when(both(crosses, later))(z_copy(up, which, head + 5).start)
 
         @pl.loop(0, frames, unroll=True)
         def _(frame):
@@ -350,10 +377,10 @@
             wait_halo(1)
 
         for up, _, _, _, receives in ways:
-            pl.when(receives)(z_copy(up, 1, head + 2).wait_recv)
-
-        @pl.loop(0, frames, unroll=True)
-        def _(frame):
+            pl.when(both(receives, head < heads - 1))(z_copy(up, 1, head + 2).wait_recv)
+            pl.when(both(receives, head == heads - 1))(z_copy(up, 1, last).wait_recv)
+
+        def attend(frame):
             near = pl.ds(frame, 3)
             total = jnp.dot(
                 weights_ref[frame, :, 9 * tokens :],
@@ -367,19 +394,26 @@
             attended = (total / denominators[frame]).astype(jnp.bfloat16)
             out_ref[frame, :, :, lanes] = attended.reshape(rows, cols, HD)
 
+        pl.loop(0, frames - 3, unroll=True)(attend)
+        for up, _, _, _, receives in ways:
+            pl.when(both(receives, head == heads - 1))(z_copy(up, 1, rest).wait_recv)
+        pl.loop(frames - 3, frames, unroll=True)(attend)
+
     for part in range(heads + 2):
         for which in range(2):
             for up, sends, _, relays, _ in ways:
                 out = jnp.logical_or(sends, relays) if relayed(part) else sends
                 pl.when(out)(z_copy(up, which, part).wait_send)
-    for slot, there in ((1, None), (0, has_low), (2, has_high)):
-        for which in range(2):
-            for forward, goes in ((True, has_after), (False, has_before)):
-                leaves = goes if there is None else both(goes, there)
-                pl.when(leaves)(t_copy(forward, which, slot).wait_send)
-    for step in range(1, tm_count):
-        for which in range(2):
-            text_copy(step, which).wait_send()
+    for up, sends, _, _, _ in ways:
+        pl.when(sends)(z_copy(up, 1, rest).wait_send)
+    for which in range(2):
+        for forward in (True, False):
+            for slot in range(3):
+                pl.when(passes_corner(forward, slot))(t_copy(forward, which, slot).wait_send)
+    for hop in range(tm_count - 1):
+        for forward, _, goes in text_ways(hop):
+            for which in range(2):
+                pl.when(goes)(text_copy(forward, which, hop).wait_send)
 
 
 def per_device(
@@ -419,12 +453,12 @@
             pltpu.VMEM((frames, tokens, tokens), jnp.float32),
             pltpu.VMEM((frames, tokens, key_total), jnp.bfloat16),
             pltpu.VMEM((frames, tokens, HD), jnp.float32),
-            pltpu.SemaphoreType.DMA((2, 2, heads + 2)),
-            pltpu.SemaphoreType.DMA((2, 2, heads + 2)),
+            pltpu.SemaphoreType.DMA((2, 2, heads + 3)),
+            pltpu.SemaphoreType.DMA((2, 2, heads + 3)),
             pltpu.SemaphoreType.DMA((2, 2, 3)),
             pltpu.SemaphoreType.DMA((2, 2, 3)),
-            pltpu.SemaphoreType.DMA((tm_count, 2)),
-            pltpu.SemaphoreType.DMA((tm_count, 2)),
+            pltpu.SemaphoreType.DMA((2, 2, tm_count)),
+            pltpu.SemaphoreType.DMA((2, 2, tm_count)),
             pltpu.SemaphoreType.DMA((7,)),
         ],
         compiler_params=pltpu.CompilerParams(

time: 79.5 us -> 78.6 us (0.989)
  Pallas kernels: 77.7 us -> 76.5 us
    pallas_call x1, Pallas kernels: 77.7 us -> 76.5 us  [per_device(): pl.pallas_call(functools.partial(kernel, tm_count, space_count), out_shap...]
where the time goes in v3:
time: 78.6 us; the launch traced here: 78.3 us
  Pallas kernels  76.5 us (97%)
  local copies, waits for them, and re-layouts  1.15 us (1%)
    pallas_call x1, Pallas kernels, per_device(): pl.pallas_call(functools.partial(kernel, tm_count, space_count), out_shap...  76.5 us

profile of v3, /device:TPU:15, one launch (start us, length us, event | category | flops | bytes accessed | tf_op | source)
XLA Modules:
  0.0 78.3 jit_solution(1127933537582941311)
XLA Ops:
  0.7 76.5 %shard_map.73 = bf16[8,4,32,768]{3,2,1,0:T(8,128)(2,1)S(1)} custom-call(s32[1]{0:T(128)S(6)} %copy.10.count_ref, s32[32,4,64]{2,1,0:T(4,128)} %bitcast.1, bf16[8,4,32,768]{3,2,1,0:T(8,128)(2,1)} %q_ref.1, bf16[8,4,32,768]{3,2,1,0:T(8,128)(2,1)} %k_ref.1, bf16[8,4,32,768]{3,2,1,0:T(8,128)(2,1)} %v_ref.1, bf16[32,768]{1,0:T(8,128)(2,1)} %text_k_ref.1, ...), custom_call_target="tpu_custom_call" | custom-call | flops 4026531840 | bytes 6291456 | tf_op jit(solution)/shard_map/pallas_call | solution.py:439
  77.1 1.1 %copy.9 = bf16[8,4,32,768]{3,2,1,0:T(8,128)(2,1)} copy(bf16[8,4,32,768]{3,2,1,0:T(8,128)(2,1)S(1)} %shard_map.73) | data formatting | bytes 3145728

commit v4 on v3

--- a/solution.py
+++ b/solution.py
@@ -43,6 +43,7 @@
     text_send,
     text_recv,
     local_sem,
+    ready,
 ):
     frames, rows, cols, feat = q_ref.shape
     heads = feat // HD
@@ -58,8 +59,6 @@
     half = space_count // 2
     crosses_up, crosses_down = s == half - 1, s == half
     relays_up, relays_down = s == space_count - 1, s == 0
-    is_middle = jnp.logical_or(crosses_up, crosses_down)
-    is_outer = jnp.logical_or(relays_up, relays_down)
     sources = ((k_ref, keys), (v_ref, values))
 
     def both(*conditions):
@@ -175,30 +174,42 @@
     def greet(where):
         pl.semaphore_signal(barrier, inc=1, device_id=where, device_id_type=MESH)
 
+    next_chip = both(lax.rem(t, 2) == 1, has_after)
+    previous_chip = both(lax.rem(t, 2) == 0, has_before)
+    hears_low = both(has_low, jnp.logical_not(crosses_down))
+    hears_after = both(has_after, jnp.logical_not(next_chip))
     pl.when(has_low)(lambda: greet({"space": low}))
-    pl.when(has_high)(lambda: greet({"space": high}))
-
-    @pl.when(is_middle)
-    def _():
-        greet({"space": 0})
-        greet({"space": space_count - 1})
-
-    @pl.when(is_outer)
+    pl.when(both(has_high, jnp.logical_not(crosses_up)))(lambda: greet({"space": high}))
+    pl.when(both(has_before, jnp.logical_not(previous_chip)))(lambda: greet({"tm": before}))
+    pl.when(has_after)(lambda: greet({"tm": after}))
+
+    @pl.when(s == 0)
     def _():
         greet({"space": half - 1})
         greet({"space": half})
 
-    pl.when(has_before)(lambda: greet({"tm": before}))
-    pl.when(has_after)(lambda: greet({"tm": after}))
+    pl.when(crosses_down)(lambda: greet({"space": space_count - 1}))
+    pl.when(s == space_count - 1)(lambda: greet({"space": half - 1}))
+
+    def number(*conditions):
+        return functools.reduce(jnp.add, [c.astype(jnp.int32) for c in conditions])
+
     pl.semaphore_wait(
         barrier,
-        has_low.astype(jnp.int32)
-        + has_high.astype(jnp.int32)
-        + 2 * is_middle.astype(jnp.int32)
-        + 2 * is_outer.astype(jnp.int32)
-        + has_before.astype(jnp.int32)
-        + has_after.astype(jnp.int32),
+        number(hears_low, has_high, has_before, hears_after)
+        + number(crosses_up, crosses_up, crosses_down, s == space_count - 1),
     )
+
+    @pl.when(crosses_up)
+    def _():
+        for where in (0, half):
+            pl.semaphore_signal(
+                ready.at[0], inc=1, device_id={"space": where}, device_id_type=MESH
+            )
+
+    @pl.when(previous_chip)
+    def _():
+        pl.semaphore_signal(ready.at[1], inc=1, device_id={"tm": before}, device_id_type=MESH)
 
     ways = (
         (True, has_high, crosses_up, relays_up, has_low),
@@ -208,29 +219,48 @@
     def relayed(part):
         return part % 2 == 0 and part >= 2
 
-    def start_part(part, through):
+    for which in range(2):
+        pl.when(hears_after)(text_copy(True, which, 0).start)
+        pl.when(has_before)(text_copy(False, which, 0).start)
+    for part in range(2):
         for which in range(2):
-            for up, sends, crosses, _, _ in ways:
-                if through:
-                    straight = both(sends, jnp.logical_not(crosses))
-                    pl.when(straight)(z_copy(up, which, part).start)
-                    pl.when(crosses)(z_copy(up, which, part, 1).start)
-                else:
-                    pl.when(sends)(z_copy(up, which, part).start)
+            pl.when(has_high)(z_copy(True, which, part).start)
+            pl.when(hears_low)(z_copy(False, which, part).start)
+
+    @pl.when(jnp.logical_or(crosses_down, s == 0))
+    def _():
+        pl.semaphore_wait(ready.at[0], 1)
+
+    @pl.when(next_chip)
+    def _():
+        pl.semaphore_wait(ready.at[1], 1)
 
     for which in range(2):
-        text_hop(which, 0)
-    start_part(0, False)
-    start_part(1, False)
+        pl.when(next_chip)(text_copy(True, which, 0).start)
+    is_outer = jnp.logical_or(s == 0, s == space_count - 1)
+
+    def text_hops():
+        for hop in range(1, tm_count):
+            for which in range(2):
+                text_hop(which, hop)
+
+    pl.when(jnp.logical_not(is_outer))(text_hops)
     for which in range(2):
         pl.when(has_after)(t_copy(True, which, 1).start)
         pl.when(has_before)(t_copy(False, which, 1).start)
+    for part in range(2):
+        for which in range(2):
+            pl.when(crosses_down)(z_copy(False, which, part).start)
 
     for part in range(2, heads + 2, 2):
-        start_part(part, True)
         for which in range(2):
             for up, sends, crosses, _, _ in ways:
-                now = sends if part == 2 else both(sends, jnp.logical_not(crosses))
+                straight = both(sends, jnp.logical_not(crosses))
+                pl.when(straight)(z_copy(up, which, part).start)
+                pl.when(crosses)(z_copy(up, which, part, 1).start)
+        for which in range(2):
+            for up, sends, crosses, _, _ in ways:
+                now = both(sends, jnp.logical_not(crosses))
                 pl.when(now)(z_copy(up, which, part + 1).start)
     for up, sends, crosses, _, _ in ways:
         pl.when(both(sends, jnp.logical_not(crosses)))(z_copy(up, 1, rest).start)
@@ -238,9 +268,7 @@
     for copy in local_copies:
         copy.start()
 
-    for hop in range(1, tm_count):
-        for which in range(2):
-            text_hop(which, hop)
+    pl.when(is_outer)(text_hops)
 
     blank = jnp.zeros((rows, cols, feat), values.dtype)
     short = jnp.zeros((rows, cols, HD), values.dtype)
@@ -335,12 +363,12 @@
         for up, _, _, _, receives in ways:
             pl.when(receives)(z_copy(up, 0, head + 2).wait_recv)
 
-        for now in range(0, heads - 2, 2):
+        for now, then in [(0, 3), (1, 5), (2, 7)]:
             for which in range(2):
                 for up, _, crosses, _, _ in ways:
-                    pl.when(both(crosses, head == now))(z_copy(up, which, now + 5).start)
+                    pl.when(both(crosses, head == now))(z_copy(up, which, then).start)
         for up, _, crosses, _, _ in ways:
-            pl.when(both(crosses, head == heads - 4))(z_copy(up, 1, rest).start)
+            pl.when(both(crosses, head == 2))(z_copy(up, 1, rest).start)
 
         @pl.when(head == 0)
         def _():
@@ -460,6 +488,7 @@
             pltpu.SemaphoreType.DMA((2, 2, tm_count)),
             pltpu.SemaphoreType.DMA((2, 2, tm_count)),
             pltpu.SemaphoreType.DMA((7,)),
+            pltpu.SemaphoreType.REGULAR((2,)),
         ],
         compiler_params=pltpu.CompilerParams(
             collective_id=0, has_side_effects=True, vmem_limit_bytes=56 * 2**20

time: 78.6 us -> 77.2 us (0.982)
  the two profiles are of different devices: /device:TPU:15 before, /device:TPU:80 now
where the time goes in v4:
time: 77.2 us; the launch traced here: 77.1 us
  Pallas kernels  75.3 us (98%)
  local copies, waits for them, and re-layouts  1.15 us (1%)
    pallas_call x1, Pallas kernels, per_device(): pl.pallas_call(functools.partial(kernel, tm_count, space_count), out_shap...  75.3 us

profile of v4, /device:TPU:80, one launch (start us, length us, event | category | flops | bytes accessed | tf_op | source)
XLA Modules:
  0.0 77.1 jit_solution(10739158289124628142)
XLA Ops:
  0.7 75.3 %shard_map.73 = bf16[8,4,32,768]{3,2,1,0:T(8,128)(2,1)S(1)} custom-call(s32[1]{0:T(128)S(6)} %copy.10.count_ref, s32[32,4,64]{2,1,0:T(4,128)} %bitcast.1, bf16[8,4,32,768]{3,2,1,0:T(8,128)(2,1)} %q_ref.1, bf16[8,4,32,768]{3,2,1,0:T(8,128)(2,1)} %k_ref.1, bf16[8,4,32,768]{3,2,1,0:T(8,128)(2,1)} %v_ref.1, bf16[32,768]{1,0:T(8,128)(2,1)} %text_k_ref.1, ...), custom_call_target="tpu_custom_call" | custom-call | flops 4026531840 | bytes 6291456 | tf_op jit(solution)/shard_map/pallas_call | solution.py:467
  76.0 1.1 %copy.9 = bf16[8,4,32,768]{3,2,1,0:T(8,128)(2,1)} copy(bf16[8,4,32,768]{3,2,1,0:T(8,128)(2,1)S(1)} %shard_map.73) | data formatting | bytes 3145728

commit v5 on v4

--- a/solution.py
+++ b/solution.py
@@ -351,6 +351,21 @@
     scale = math.log2(math.e) / math.sqrt(HD)
     text_allowed = lax.broadcasted_iota(jnp.int32, (tokens, text_total), 1) < count[0]
 
+    def wait_sent():
+        for part in range(last):
+            for which in range(2):
+                for up, sends, _, relays, _ in ways:
+                    out = jnp.logical_or(sends, relays) if relayed(part) else sends
+                    pl.when(out)(z_copy(up, which, part).wait_send)
+        for which in range(2):
+            for forward in (True, False):
+                for slot in range(3):
+                    pl.when(passes_corner(forward, slot))(t_copy(forward, which, slot).wait_send)
+        for hop in range(tm_count - 1):
+            for forward, _, goes in text_ways(hop):
+                for which in range(2):
+                    pl.when(goes)(text_copy(forward, which, hop).wait_send)
+
     @pl.loop(0, heads)
     def _(head):
         lanes = pl.ds(pl.multiple_of(head * HD, HD), HD)
@@ -404,6 +419,7 @@
         def _():
             wait_halo(1)
 
+        pl.when(head == heads - 1)(wait_sent)
         for up, _, _, _, receives in ways:
             pl.when(both(receives, head < heads - 1))(z_copy(up, 1, head + 2).wait_recv)
             pl.when(both(receives, head == heads - 1))(z_copy(up, 1, last).wait_recv)
@@ -427,22 +443,13 @@
             pl.when(both(receives, head == heads - 1))(z_copy(up, 1, rest).wait_recv)
         pl.loop(frames - 3, frames, unroll=True)(attend)
 
-    for part in range(heads + 2):
+    for part in range(last, heads + 2):
         for which in range(2):
             for up, sends, _, relays, _ in ways:
                 out = jnp.logical_or(sends, relays) if relayed(part) else sends
                 pl.when(out)(z_copy(up, which, part).wait_send)
     for up, sends, _, _, _ in ways:
         pl.when(sends)(z_copy(up, 1, rest).wait_send)
-    for which in range(2):
-        for forward in (True, False):
-            for slot in range(3):
-                pl.when(passes_corner(forward, slot))(t_copy(forward, which, slot).wait_send)
-    for hop in range(tm_count - 1):
-        for forward, _, goes in text_ways(hop):
-            for which in range(2):
-                pl.when(goes)(text_copy(forward, which, hop).wait_send)
-
 
 def per_device(
     tm_count,

time: 77.2 us -> 77.2 us (level)
  the two profiles are of different devices: /device:TPU:80 before, /device:TPU:70 now
where the time goes in v5:
time: 77.2 us; the launch traced here: 77.1 us
  Pallas kernels  75.3 us (98%)
  local copies, waits for them, and re-layouts  1.15 us (1%)
    pallas_call x1, Pallas kernels, per_device(): pl.pallas_call(functools.partial(kernel, tm_count, space_count), out_shap...  75.3 us

profile of v5, /device:TPU:70, one launch (start us, length us, event | category | flops | bytes accessed | tf_op | source)
XLA Modules:
  0.0 77.1 jit_solution(8327624728784105880)
XLA Ops:
  0.7 75.3 %shard_map.73 = bf16[8,4,32,768]{3,2,1,0:T(8,128)(2,1)S(1)} custom-call(s32[1]{0:T(128)S(6)} %copy.10.count_ref, s32[32,4,64]{2,1,0:T(4,128)} %bitcast.1, bf16[8,4,32,768]{3,2,1,0:T(8,128)(2,1)} %q_ref.1, bf16[8,4,32,768]{3,2,1,0:T(8,128)(2,1)} %k_ref.1, bf16[8,4,32,768]{3,2,1,0:T(8,128)(2,1)} %v_ref.1, bf16[32,768]{1,0:T(8,128)(2,1)} %text_k_ref.1, ...), custom_call_target="tpu_custom_call" | custom-call | flops 4026531840 | bytes 6291456 | tf_op jit(solution)/shard_map/pallas_call | solution.py:474
  75.9 1.1 %copy.9 = bf16[8,4,32,768]{3,2,1,0:T(8,128)(2,1)} copy(bf16[8,4,32,768]{3,2,1,0:T(8,128)(2,1)S(1)} %shard_map.73) | data formatting | bytes 3145728
